TPU v7x, 256 devices: a whole 4x4x8 slice. The times are simulated.
256 devices in a mesh: snap: 16 (over z, core), vtx: 16 (over y, x).
Axes of the slice: x: 4, y: 4, z: 8, core: 2. Of those that a mesh axis runs over, the one named last changes fastest.
Arguments:
- feats: float32 [16, 16384, 512], P('snap', 'vtx'), may hold values from -6 to 6
- col_ids: int32 [16, 128, 16], P('snap', 'vtx'), may hold values from 0 to 127
- tiles: float32 [16, 128, 16, 128, 128], P('snap', 'vtx'), may hold values from -0.125 to 0.125
- w_first: float32 [512, 256], replicated, may hold values from -0.25 to 0.25
- w_input: float32 [256, 1024], replicated, may hold values from -0.375 to 0.375
- w_recur: float32 [256, 1024], replicated, may hold values from -0.375 to 0.375
- lstm_bias: float32 [1024], replicated, may hold values from -3 to 3
- w_second: float32 [256, 256], replicated, may hold values from -0.375 to 0.375
Outputs:
- output: float32 [16, 16384, 256], P('snap', 'vtx')
Inputs may be any that keep to these rules, and one draw needn't show every extreme that they name: `col_ids`: every entry names a row block of the same snapshot's graph; a few blocks are named far more often than others.
All inputs are finite; a program needn't handle non-finite values.
Results may differ from a plain program's by a relative error of at most 0.0003.
Values sent between devices are 32-bit elements; how exact they have to be, the bound alone decides.
A program may use at most 128 MiB of HBM per device.

v0:
```python
import jax
import jax.numpy as jnp
from jax import lax
from jax.sharding import PartitionSpec as P


def block_sum(tile_set, column_ids, source):
    tile_edge = tile_set.shape[-1]
    width = source.shape[-1]
    blocks = source.reshape(source.shape[0] // tile_edge, tile_edge, width)

    def row_block(operands):
        tiles_here, ids_here = operands
        picked = blocks[ids_here]
        return jnp.einsum("ktu,kuw->tw", tiles_here, picked, precision=lax.Precision.HIGHEST)

    summed = lax.map(row_block, (tile_set, column_ids))
    return summed.reshape(-1, width)


def row_scale(tiles):
    sums = jnp.sum(tiles * tiles, axis=(2, 4))
    return lax.rsqrt(1.0 + sums).reshape(tiles.shape[0], -1)[..., None]


def recurrence(pre_time, w_recur, lstm_bias):
    hidden_size = w_recur.shape[0]

    def advance(carry, pre_step):
        state_h, state_c = carry
        gates = pre_step + jnp.dot(state_h, w_recur, precision=lax.Precision.HIGHEST) + lstm_bias
        gate_i = gates[:, :hidden_size]
        gate_f = gates[:, hidden_size : 2 * hidden_size]
        gate_g = gates[:, 2 * hidden_size : 3 * hidden_size]
        gate_o = gates[:, 3 * hidden_size :]
        state_c = jax.nn.sigmoid(gate_f) * state_c + jax.nn.sigmoid(gate_i) * jnp.tanh(gate_g)
        state_h = jax.nn.sigmoid(gate_o) * jnp.tanh(state_c)
        return ((state_h, state_c), state_h)

    zeros = jnp.zeros((pre_time.shape[1], hidden_size), jnp.float32)
    _, states = lax.scan(advance, (zeros, zeros), pre_time)
    return states


def on_device(feats, col_ids, tiles, w_first, w_input, w_recur, lstm_bias, w_second):
    scale = row_scale(tiles)
    whole = lax.all_gather(feats, "vtx", axis=1, tiled=True)
    mixed = scale * (feats + jax.vmap(block_sum)(tiles, col_ids, whole))
    hidden_one = jax.nn.relu(
        jnp.einsum("svf,fh->svh", mixed, w_first, precision=lax.Precision.HIGHEST)
    )
    timelines = lax.all_to_all(hidden_one, "snap", split_axis=1, concat_axis=0, tiled=True)
    pre_time = jnp.einsum("svh,hg->svg", timelines, w_input, precision=lax.Precision.HIGHEST)
    states = recurrence(pre_time, w_recur, lstm_bias)
    returned = lax.all_to_all(states, "snap", split_axis=0, concat_axis=1, tiled=True)
    whole_two = lax.all_gather(returned, "vtx", axis=1, tiled=True)
    mixed_two = scale * (returned + jax.vmap(block_sum)(tiles, col_ids, whole_two))
    return jnp.einsum("svh,hg->svg", mixed_two, w_second, precision=lax.Precision.HIGHEST)


def solution(mesh):
    placed = (
        P("snap", "vtx", None),
        P("snap", "vtx", None),
        P("snap", "vtx", None, None, None),
        P(),
        P(),
        P(),
        P(),
        P(),
    )
    return jax.shard_map(
        on_device, mesh=mesh, in_specs=placed, out_specs=P("snap", "vtx", None), check_vma=False
    )
```

profile of v0, /device:TPU:1, one launch (start us, length us, event | category | flops | bytes accessed | tf_op | source)
XLA Modules:
  0.0 617.5 jit_solution(13330983946178340313)
XLA Ops:
  7.3 4.0 multiply_reduce_fusion
  11.3 204.4 %all-gather.3.cloned.1.call-done = f32[1,16384,512]{2,1,0:T(8,128)} async-done(((f32[1,1024,512]{2,1,0:T(8,128)}), f32[1,16384,512]{2,1,0:T(8,128)}) %all-gather.3.cloned.1.call-update) | async-done | bytes 33554448 | tf_op jit(solution)/shard_map/all_gather | solution.py:47
  215.7 91.2 %while.35 = (s32[]{:T(128)}, f32[8,1,128,512]{3,2,1,0:T(8,128)}, f32[8,1,16,128,128]{4,3,2,1,0:T(8,128)}, s32[8,1,16]{2,1,0:T(1,128)}, f32[1,128,128,512]{3,2,1,0:T(8,128)}, /*index=5*/s32[]{:T(128)}) while((s32[]{:T(128)}, f32[8,1,128,512]{3,2,1,0:T(8,128)}, f32[8,1,16,128,128]{4,3,2,1,0:T(8,128)}, s32[8,1,16]{2,1,0:T(1,128)}, ...), condition=%wide.region_2.3_spmd, body=%wide.region_1.2_spmd.sunk | while | flops 1610612864 | bytes 13895369 | solution.py:17
  216.5 5.1 gather_fusion
  221.6 5.7 fusion.62
  227.9 5.0 gather_fusion
  232.9 5.7 fusion.62
  239.3 5.0 gather_fusion
  244.3 5.7 fusion.62
  250.6 5.1 gather_fusion
  255.7 5.7 fusion.62
  262.1 5.1 gather_fusion
  267.2 5.6 fusion.62
  273.5 5.1 gather_fusion
  278.6 5.6 fusion.62
  284.9 5.0 gather_fusion
  289.9 5.6 fusion.62
  296.2 5.0 gather_fusion
  301.2 5.7 fusion.62
  306.9 3.5 fusion.35
  310.4 2.0 copy.12
  312.5 7.8 %all-to-all-start = ((f32[1,1024,256]{2,0,1:T(1,128)}), f32[1,1024,256]{2,0,1:T(1,128)S(1)}, u32[]{:S(2)}, u32[]{:S(2)}) async-start(f32[1,1024,256]{2,0,1:T(1,128)} %copy.12), calls=%async_computation | async-start | bytes 2097152 | tf_op jit(solution)/shard_map/all_to_all | solution.py:52
  320.4 27.9 %all-to-all-done = f32[1,1024,256]{2,0,1:T(1,128)S(1)} async-done(((f32[1,1024,256]{2,0,1:T(1,128)}), f32[1,1024,256]{2,0,1:T(1,128)S(1)}, u32[]{:S(2)}, u32[]{:S(2)}) %all-to-all-start) | async-done | bytes 1048608 | tf_op jit(solution)/shard_map/all_to_all | solution.py:52
  348.3 5.0 fusion.39
  353.3 29.0 %while.37 = (s32[]{:T(128)}, f32[64,256]{1,0:T(8,128)S(1)}, f32[64,256]{1,0:T(8,128)S(1)}, f32[16,64,256]{2,1,0:T(8,128)S(1)}, f32[16,64,1024]{2,1,0:T(8,128)}, ...) while((s32[]{:T(128)}, f32[64,256]{1,0:T(8,128)S(1)}, ...), condition=%wide.region_4.5_spmd.clone, body=%wide.region_3.4_spmd.clone.sunk | while | flops 201703424 | bytes 2166896 | solution.py:41
  355.1 1.7 fusion.68
  378.8 1.7 fusion.68
  382.4 32.0 %all_to_all.27 = f32[16,64,256]{2,1,0:T(8,128)} all-to-all(f32[16,64,256]{2,1,0:T(8,128)S(1)} %get-tuple-element.97), channel_id=1, replica_groups=mesh['snap'=16,'vtx'=16] {'snap'}, dimensions={0} | all-to-all | bytes 2097152 | tf_op jit(solution)/shard_map/all_to_all | solution.py:55
  414.4 111.3 %all-gather.5.cloned.1.call-done = f32[1,16384,256]{2,1,0:T(8,128)} async-done(((f32[1,1024,256]{2,1,0:T(8,128)}), f32[1,16384,256]{2,1,0:T(8,128)}) %all-gather.5.cloned.1.call-update) | async-done | bytes 16777232 | tf_op jit(solution)/shard_map/all_gather | solution.py:56
  525.7 81.2 %while.36 = (s32[]{:T(128)}, f32[8,1,128,256]{3,2,1,0:T(8,128)}, f32[8,1,16,128,128]{4,3,2,1,0:T(8,128)}, s32[8,1,16]{2,1,0:T(1,128)}, f32[1,128,128,256]{3,2,1,0:T(8,128)}, /*index=5*/s32[]{:T(128)}) while((s32[]{:T(128)}, f32[8,1,128,256]{3,2,1,0:T(8,128)}, f32[8,1,16,128,128]{4,3,2,1,0:T(8,128)}, s32[8,1,16]{2,1,0:T(1,128)}, ...), condition=%wide.region_6.7_spmd, body=%wide.region_5.6_spmd.sunk | while | flops 805306496 | bytes 7472841 | solution.py:17
  526.4 6.4 %gather_fusion.1 = f32[16,128,256]{2,1,0:T(8,128)S(1)} fusion(f32[1,128,128,256]{3,2,1,0:T(8,128)} %get-tuple-element.352, s32[16]{0:T(128)S(1)} %or_bitcast_fusion.5), kind=kCustom, calls=%fused_computation.1.clone.1 | custom fusion | bytes 4194432 | tf_op jit(solution)/shard_map/vmap()/while/body/eval_jaxpr/gather | solution.py:14
  532.8 3.0 fusion.65
  536.5 6.4 %gather_fusion.1 = f32[16,128,256]{2,1,0:T(8,128)S(1)} fusion(f32[1,128,128,256]{3,2,1,0:T(8,128)} %get-tuple-element.352, s32[16]{0:T(128)S(1)} %or_bitcast_fusion.5), kind=kCustom, calls=%fused_computation.1.clone.1 | custom fusion | bytes 4194432 | tf_op jit(solution)/shard_map/vmap()/while/body/eval_jaxpr/gather | solution.py:14
  543.0 3.0 fusion.65
  546.7 6.4 %gather_fusion.1 = f32[16,128,256]{2,1,0:T(8,128)S(1)} fusion(f32[1,128,128,256]{3,2,1,0:T(8,128)} %get-tuple-element.352, s32[16]{0:T(128)S(1)} %or_bitcast_fusion.5), kind=kCustom, calls=%fused_computation.1.clone.1 | custom fusion | bytes 4194432 | tf_op jit(solution)/shard_map/vmap()/while/body/eval_jaxpr/gather | solution.py:14
  553.1 3.0 fusion.65
  556.8 6.4 %gather_fusion.1 = f32[16,128,256]{2,1,0:T(8,128)S(1)} fusion(f32[1,128,128,256]{3,2,1,0:T(8,128)} %get-tuple-element.352, s32[16]{0:T(128)S(1)} %or_bitcast_fusion.5), kind=kCustom, calls=%fused_computation.1.clone.1 | custom fusion | bytes 4194432 | tf_op jit(solution)/shard_map/vmap()/while/body/eval_jaxpr/gather | solution.py:14
  563.3 3.0 fusion.65
  567.0 6.4 %gather_fusion.1 = f32[16,128,256]{2,1,0:T(8,128)S(1)} fusion(f32[1,128,128,256]{3,2,1,0:T(8,128)} %get-tuple-element.352, s32[16]{0:T(128)S(1)} %or_bitcast_fusion.5), kind=kCustom, calls=%fused_computation.1.clone.1 | custom fusion | bytes 4194432 | tf_op jit(solution)/shard_map/vmap()/while/body/eval_jaxpr/gather | solution.py:14
  573.4 3.0 fusion.65
  577.1 6.4 %gather_fusion.1 = f32[16,128,256]{2,1,0:T(8,128)S(1)} fusion(f32[1,128,128,256]{3,2,1,0:T(8,128)} %get-tuple-element.352, s32[16]{0:T(128)S(1)} %or_bitcast_fusion.5), kind=kCustom, calls=%fused_computation.1.clone.1 | custom fusion | bytes 4194432 | tf_op jit(solution)/shard_map/vmap()/while/body/eval_jaxpr/gather | solution.py:14
  583.6 3.0 fusion.65
  587.3 6.4 %gather_fusion.1 = f32[16,128,256]{2,1,0:T(8,128)S(1)} fusion(f32[1,128,128,256]{3,2,1,0:T(8,128)} %get-tuple-element.352, s32[16]{0:T(128)S(1)} %or_bitcast_fusion.5), kind=kCustom, calls=%fused_computation.1.clone.1 | custom fusion | bytes 4194432 | tf_op jit(solution)/shard_map/vmap()/while/body/eval_jaxpr/gather | solution.py:14
  593.7 3.0 fusion.65
  597.4 6.4 %gather_fusion.1 = f32[16,128,256]{2,1,0:T(8,128)S(1)} fusion(f32[1,128,128,256]{3,2,1,0:T(8,128)} %get-tuple-element.352, s32[16]{0:T(128)S(1)} %or_bitcast_fusion.5), kind=kCustom, calls=%fused_computation.1.clone.1 | custom fusion | bytes 4194432 | tf_op jit(solution)/shard_map/vmap()/while/body/eval_jaxpr/gather | solution.py:14
  603.9 3.0 fusion.65
  606.9 1.8 fusion.38
  608.7 2.0 convolution_bitcast_fusion.2
  (99 shorter events, 37.1 us)
Async XLA Ops:
  6.5 341.8 %copy-start = (f32[256,1024]{1,0:T(8,128)S(1)}, f32[256,1024]{1,0:T(8,128)}, u32[]{:S(2)}) copy-start(f32[256,1024]{1,0:T(8,128)} %param.18) | copy-start | bytes 3145732
  6.5 209.2 %all-gather.3.cloned.1.call-start = ((), (), s32[]{:S(2)}) async-start(), calls=%async_computation.2 | async-start | bytes 35651584 | tf_op jit(solution)/shard_map/all_gather | solution.py:47
  215.7 91.2 %copy-start.2 = (f32[1,1024,512]{2,1,0:T(8,128)S(1)}, f32[1,1024,512]{2,1,0:T(8,128)}, u32[]{:S(2)}) copy-start(f32[1,1024,512]{2,1,0:T(8,128)} %param.14) | copy-start | bytes 6291460
  312.5 35.7 %all-to-all-start = ((f32[1,1024,256]{2,0,1:T(1,128)}), f32[1,1024,256]{2,0,1:T(1,128)S(1)}, u32[]{:S(2)}, u32[]{:S(2)}) async-start(f32[1,1024,256]{2,0,1:T(1,128)} %copy.12), calls=%async_computation | async-start | bytes 2097152 | tf_op jit(solution)/shard_map/all_to_all | solution.py:52
  320.3 205.4 %all-gather.5.cloned.1.call-start = ((), (), s32[]{:S(2)}) async-start(), calls=%async_computation.3 | async-start | bytes 17825792 | tf_op jit(solution)/shard_map/all_gather | solution.py:56
  348.3 5.0 copy-start.1
  348.3 5.0 copy-start.4
  606.9 1.8 copy-start.3
Sparse Core Ops, SparseCore 0:
  9.8 205.8 all-gather.2
  414.5 111.1 all-gather.4
where the time goes:
time: 619 us; the launch traced here: 617 us
  waiting for transfers between devices  344 us (56%)
  matrix products  107 us (17%)
  local copies, waits for them, and re-layouts  94.3 us (15%)
  blocking collectives  32 us (5%)
  other arithmetic  18 us (3%)
  between operations  13.5 us (2%)
  starting transfers between devices  7.85 us (1%)
    all_gather x1, waiting for transfers between devices, on_device(): whole = lax.all_gather(feats, 'vtx', axis=1, tiled=True)  204 us
    all_gather x1, waiting for transfers between devices, on_device(): whole_two = lax.all_gather(returned, 'vtx', axis=1, tiled=True)  111 us
    gather x32, local copies, waits for them, and re-layouts, row_block(): picked = blocks[ids_here]  92.1 us
    dot_general x16, matrix products, row_block(): jnp.einsum('ktu,kuw->tw', tiles_here, picked, precision=lax.Precision.HIG...  69.3 us
    all_to_all x1, blocking collectives, on_device(): lax.all_to_all(states, 'snap', split_axis=0, concat_axis=1, tiled=True)  32 us
    all_to_all x1, waiting for transfers between devices, on_device(): lax.all_to_all(hidden_one, 'snap', split_axis=1, concat_axis=0, tiled=True)  27.9 us
    dot_general x16, matrix products, advance(): jnp.dot(state_h, w_recur, precision=lax.Precision.HIGHEST)  27.3 us
  transfers between devices with their start and end apart: 3, of which 3 were waited for; matrix products, arithmetic and copies ran while one was open for 1% of the time, Pallas kernels for 0%

commit v1 on v0

--- a/solution.py
+++ b/solution.py
@@ -53,7 +53,37 @@
     pre_time = jnp.einsum("svh,hg->svg", timelines, w_input, precision=lax.Precision.HIGHEST)
     states = recurrence(pre_time, w_recur, lstm_bias)
     returned = lax.all_to_all(states, "snap", split_axis=0, concat_axis=1, tiled=True)
-    whole_two = lax.all_gather(returned, "vtx", axis=1, tiled=True)
+    arr_out = lax.axis_size("vtx")
+    mixed_arr = lax.axis_index("vtx")
+    part_now, inter, out_arr = (arr_out, mixed_arr, returned.shape[1])
+    rows = []
+    rr = 0
+    while rr < part_now:
+        rows.append((rr, (rr + 1) % part_now))
+        rr += 1
+    fields = []
+    rr = 0
+    while rr < part_now:
+        fields.append((rr, (rr - 1) % part_now))
+        rr = rr + 1
+    whole_two = jnp.zeros(
+        (*returned.shape[:1], part_now * out_arr, *returned.shape[1 + 1 :]), returned.dtype
+    )
+    whole_two = lax.dynamic_update_slice_in_dim(whole_two, returned, inter * out_arr, axis=1)
+    local_next = t_next = returned
+    val2 = part_now // 2
+    to_i = 1
+    while to_i < val2 + 1:
+        local_next = lax.ppermute(local_next, "vtx", rows)
+        whole_two = lax.dynamic_update_slice_in_dim(
+            whole_two, local_next, (inter - to_i) % part_now * out_arr, axis=1
+        )
+        if to_i < part_now - val2:
+            t_next = lax.ppermute(t_next, "vtx", fields)
+            whole_two = lax.dynamic_update_slice_in_dim(
+                whole_two, t_next, (inter + to_i) % part_now * out_arr, axis=1
+            )
+        to_i = to_i + 1
     mixed_two = scale * (returned + jax.vmap(block_sum)(tiles, col_ids, whole_two))
     return jnp.einsum("svh,hg->svg", mixed_two, w_second, precision=lax.Precision.HIGHEST)
 

time: 619 us -> 734 us (1.19)
  waiting for transfers between devices: 344 us -> 397 us
  starting transfers between devices: 7.85 us -> 41.8 us
  local copies, waits for them, and re-layouts: 94.3 us -> 109 us
  other arithmetic: 18 us -> 28.1 us
    ppermute x0 -> x15, waiting for transfers between devices: none -> 164 us  [the longest x8 164 us: on_device(): local_next = lax.ppermute(local_next, 'vtx', rows)]
    all_gather x1 -> x0, waiting for transfers between devices: 111 us -> none  [on_device(): whole_two = lax.all_gather(returned, 'vtx', axis=1, tiled=True)]
    ppermute x0 -> x15, starting transfers between devices: none -> 33.9 us  [the longest x7 33 us: on_device(): t_next = lax.ppermute(t_next, 'vtx', fields)]
    dynamic_update_slice x16, other arithmetic: 1.36 us -> 11.5 us  [recurrence(): _, states = lax.scan(advance, (zeros, zeros), pre_time)]
    unnamed x11 -> x47, local copies, waits for them, and re-layouts: 0.09 us -> 7.44 us
  transfers between devices with their start and end apart: 3 -> 17, of which waited for: 3 -> 10; matrix products, arithmetic and copies ran while one was open for 1% -> 2% of each run, Pallas kernels for 0% -> 0%
where the time goes in v1:
time: 734 us; the launch traced here: 730 us
  waiting for transfers between devices  397 us (54%)
  local copies, waits for them, and re-layouts  109 us (15%)
  matrix products  108 us (15%)
  starting transfers between devices  41.8 us (6%)
  blocking collectives  32.1 us (4%)
  other arithmetic  28.1 us (4%)
  between operations  13.8 us (2%)
    all_gather x1, waiting for transfers between devices, on_device(): whole = lax.all_gather(feats, 'vtx', axis=1, tiled=True)  204 us
    ppermute x8, waiting for transfers between devices, on_device(): local_next = lax.ppermute(local_next, 'vtx', rows)  164 us
    gather x32, local copies, waits for them, and re-layouts, row_block(): picked = blocks[ids_here]  92.3 us
    dot_general x16, matrix products, row_block(): jnp.einsum('ktu,kuw->tw', tiles_here, picked, precision=lax.Precision.HIG...  69.4 us
    ppermute x7, starting transfers between devices, on_device(): t_next = lax.ppermute(t_next, 'vtx', fields)  33 us
    all_to_all x1, blocking collectives, on_device(): lax.all_to_all(states, 'snap', split_axis=0, concat_axis=1, tiled=True)  32.1 us
    all_to_all x1, waiting for transfers between devices, on_device(): lax.all_to_all(hidden_one, 'snap', split_axis=1, concat_axis=0, tiled=True)  27.9 us
    dot_general x16, matrix products, advance(): jnp.dot(state_h, w_recur, precision=lax.Precision.HIGHEST)  27.3 us
  transfers between devices with their start and end apart: 17, of which 10 were waited for; matrix products, arithmetic and copies ran while one was open for 2% of the time, Pallas kernels for 0%

profile of v1, /device:TPU:1, one launch (start us, length us, event | category | flops | bytes accessed | tf_op | source)
XLA Modules:
  0.0 729.5 jit_solution(17671376433136983278)
XLA Ops:
  11.3 204.4 %all-gather.2.cloned.1.call-done = f32[1,16384,512]{2,1,0:T(8,128)} async-done(((f32[1,1024,512]{2,1,0:T(8,128)}), f32[1,16384,512]{2,1,0:T(8,128)}) %all-gather.2.cloned.1.call-update) | async-done | bytes 33554448 | tf_op jit(solution)/shard_map/all_gather | solution.py:47
  215.7 91.3 %while.35 = (s32[]{:T(128)}, f32[8,1,128,512]{3,2,1,0:T(8,128)}, f32[8,1,16,128,128]{4,3,2,1,0:T(8,128)}, s32[8,1,16]{2,1,0:T(1,128)}, f32[1,128,128,512]{3,2,1,0:T(8,128)}, /*index=5*/s32[]{:T(128)}) while((s32[]{:T(128)}, f32[8,1,128,512]{3,2,1,0:T(8,128)}, f32[8,1,16,128,128]{4,3,2,1,0:T(8,128)}, s32[8,1,16]{2,1,0:T(1,128)}, ...), condition=%wide.region_2.3_spmd, body=%wide.region_1.2_spmd.sunk | while | flops 1610612864 | bytes 13895369 | solution.py:17
  216.4 5.1 gather_fusion
  221.5 5.7 fusion.62
  227.9 5.0 gather_fusion
  232.9 5.7 fusion.62
  239.2 5.1 gather_fusion
  244.3 5.6 fusion.62
  250.7 5.1 gather_fusion
  255.8 5.7 fusion.62
  262.1 5.0 gather_fusion
  267.1 5.7 fusion.62
  273.5 5.2 gather_fusion
  278.6 5.7 fusion.62
  285.0 5.0 gather_fusion
  290.0 5.7 fusion.62
  296.4 5.0 gather_fusion
  301.4 5.7 fusion.62
  307.0 4.2 fusion.35
  313.3 7.8 %all-to-all-start = ((f32[1,1024,256]{2,0,1:T(1,128)}), f32[1,1024,256]{2,0,1:T(1,128)S(1)}, u32[]{:S(2)}, u32[]{:S(2)}) async-start(f32[1,1024,256]{2,0,1:T(1,128)} %copy.12), calls=%async_computation | async-start | bytes 2097152 | tf_op jit(solution)/shard_map/all_to_all | solution.py:52
  321.1 27.9 %all-to-all-done = f32[1,1024,256]{2,0,1:T(1,128)S(1)} async-done(((f32[1,1024,256]{2,0,1:T(1,128)}), f32[1,1024,256]{2,0,1:T(1,128)S(1)}, u32[]{:S(2)}, u32[]{:S(2)}) %all-to-all-start) | async-done | bytes 1048608 | tf_op jit(solution)/shard_map/all_to_all | solution.py:52
  349.1 5.1 fusion.39
  354.2 38.8 %while.37 = (s32[]{:T(128)}, f32[64,256]{1,0:T(8,128)S(1)}, f32[64,256]{1,0:T(8,128)S(1)}, f32[16,64,256]{2,1,0:T(8,128)}, f32[16,64,1024]{2,1,0:T(8,128)}, /*in...) while((s32[]{:T(128)}, f32[64,256]{1,0:T(8,128)S(1)}, ...), condition=%wide.region_4.5_spmd.clone, body=%wide.region_3.4_spmd.clone.sunk | while | flops 201703424 | bytes 2167404 | solution.py:41
  393.0 32.1 %all_to_all.27 = f32[16,64,256]{2,1,0:T(8,128)S(1)} all-to-all(f32[16,64,256]{2,1,0:T(8,128)} %get-tuple-element.97), channel_id=1, replica_groups=mesh['snap'=16,'vtx'=16] {'snap'}, dimensions={0} | all-to-all | bytes 2097152 | tf_op jit(solution)/shard_map/all_to_all | solution.py:55
  429.9 22.7 %collective-permute-done = f32[1,1024,256]{2,1,0:T(8,128)S(1)} collective-permute-done((f32[1,1024,256]{2,1,0:T(8,128)S(1)}, f32[1,1024,256]{2,1,0:T(8,128)S(1)}, u32[]{:S(2)}, u32[]{:S(2)}) %collective-permute-start) | collective-permute-done | bytes 1048608 | tf_op jit(solution)/shard_map/ppermute | solution.py:77
  452.6 5.1 collective-permute-start.3
  457.6 23.1 %collective-permute-done.2 = f32[1,1024,256]{2,1,0:T(8,128)S(1)} collective-permute-done((f32[1,1024,256]{2,1,0:T(8,128)S(1)}, f32[1,1024,256]{2,1,0:T(8,128)S(1)}, u32[]{:S(2)}, u32[]{:S(2)}) %collective-permute-start.2) | collective-permute-done | bytes 1048608 | tf_op jit(solution)/shard_map/ppermute | solution.py:77
  480.7 4.8 collective-permute-start.5
  485.5 22.4 %collective-permute-done.4 = f32[1,1024,256]{2,1,0:T(8,128)S(1)} collective-permute-done((f32[1,1024,256]{2,1,0:T(8,128)S(1)}, f32[1,1024,256]{2,1,0:T(8,128)S(1)}, u32[]{:S(2)}, u32[]{:S(2)}) %collective-permute-start.4) | collective-permute-done | bytes 1048608 | tf_op jit(solution)/shard_map/ppermute | solution.py:77
  507.9 4.8 collective-permute-start.7
  512.8 21.4 %collective-permute-done.6 = f32[1,1024,256]{2,1,0:T(8,128)S(1)} collective-permute-done((f32[1,1024,256]{2,1,0:T(8,128)S(1)}, f32[1,1024,256]{2,1,0:T(8,128)S(1)}, u32[]{:S(2)}, u32[]{:S(2)}) %collective-permute-start.6) | collective-permute-done | bytes 1048608 | tf_op jit(solution)/shard_map/ppermute | solution.py:77
  535.2 4.8 collective-permute-start.9
  540.0 20.6 %collective-permute-done.8 = f32[1,1024,256]{2,1,0:T(8,128)S(1)} collective-permute-done((f32[1,1024,256]{2,1,0:T(8,128)S(1)}, f32[1,1024,256]{2,1,0:T(8,128)S(1)}, u32[]{:S(2)}, u32[]{:S(2)}) %collective-permute-start.8) | collective-permute-done | bytes 1048608 | tf_op jit(solution)/shard_map/ppermute | solution.py:77
  560.6 4.8 collective-permute-start.11
  565.5 19.7 %collective-permute-done.10 = f32[1,1024,256]{2,1,0:T(8,128)} collective-permute-done((f32[1,1024,256]{2,1,0:T(8,128)S(1)}, f32[1,1024,256]{2,1,0:T(8,128)}, u32[]{:S(2)}, u32[]{:S(2)}) %collective-permute-start.10) | collective-permute-done | bytes 1048608 | tf_op jit(solution)/shard_map/ppermute | solution.py:77
  587.4 4.9 collective-permute-start.13
  592.4 16.7 %collective-permute-done.12 = f32[1,1024,256]{2,1,0:T(8,128)} collective-permute-done((f32[1,1024,256]{2,1,0:T(8,128)}, f32[1,1024,256]{2,1,0:T(8,128)}, u32[]{:S(2)}, u32[]{:S(2)}) %collective-permute-start.12) | collective-permute-done | bytes 1048608 | tf_op jit(solution)/shard_map/ppermute | solution.py:77
  614.6 17.2 %collective-permute-done.14 = f32[1,1024,256]{2,1,0:T(8,128)S(1)} collective-permute-done((f32[1,1024,256]{2,1,0:T(8,128)}, f32[1,1024,256]{2,1,0:T(8,128)S(1)}, u32[]{:S(2)}, u32[]{:S(2)}) %collective-permute-start.14) | collective-permute-done | bytes 1048608 | tf_op jit(solution)/shard_map/ppermute | solution.py:77
  632.0 5.8 copy-done.1
  637.7 81.2 %while.36 = (s32[]{:T(128)}, f32[8,1,128,256]{3,2,1,0:T(8,128)}, f32[8,1,16,128,128]{4,3,2,1,0:T(8,128)}, s32[8,1,16]{2,1,0:T(1,128)}, f32[1,128,128,256]{3,2,1,0:T(8,128)}, /*index=5*/s32[]{:T(128)}) while((s32[]{:T(128)}, f32[8,1,128,256]{3,2,1,0:T(8,128)}, f32[8,1,16,128,128]{4,3,2,1,0:T(8,128)}, s32[8,1,16]{2,1,0:T(1,128)}, ...), condition=%wide.region_6.7_spmd, body=%wide.region_5.6_spmd.sunk | while | flops 805306496 | bytes 7472841 | solution.py:17
  638.4 6.4 gather_fusion.1
  648.6 6.4 gather_fusion.1
  658.7 6.4 gather_fusion.1
  668.9 6.4 gather_fusion.1
  679.0 6.4 gather_fusion.1
  689.2 6.4 gather_fusion.1
  699.3 6.4 gather_fusion.1
  709.5 6.4 gather_fusion.1
  (179 shorter events, 98.1 us)
Async XLA Ops:
  6.5 342.6 %copy-start = (f32[256,1024]{1,0:T(8,128)S(1)}, f32[256,1024]{1,0:T(8,128)}, u32[]{:S(2)}) copy-start(f32[256,1024]{1,0:T(8,128)} %param.18) | copy-start | bytes 3145732
  6.5 209.2 %all-gather.2.cloned.1.call-start = ((), (), s32[]{:S(2)}) async-start(), calls=%async_computation.2 | async-start | bytes 35651584 | tf_op jit(solution)/shard_map/all_gather | solution.py:47
  215.7 91.3 %copy-start.20 = (f32[512,256]{1,0:T(8,128)S(1)}, f32[512,256]{1,0:T(8,128)}, u32[]{:S(2)}) copy-start(f32[512,256]{1,0:T(8,128)} %param.17) | copy-start | bytes 1572868
  307.0 47.2 %copy-start.2 = (f32[256,1024]{1,0:T(8,128)S(1)}, f32[256,1024]{1,0:T(8,128)}, u32[]{:S(2)}) copy-start(f32[256,1024]{1,0:T(8,128)} %param.19) | copy-start | bytes 3145732
  307.0 47.2 %copy-start.22 = (f32[1024]{0:T(1024)S(1)}, f32[1024]{0:T(1024)}, u32[]{:S(2)}) copy-start(f32[1024]{0:T(1024)} %param.20) | copy-start | bytes 12292
  313.3 35.8 %all-to-all-start = ((f32[1,1024,256]{2,0,1:T(1,128)}), f32[1,1024,256]{2,0,1:T(1,128)S(1)}, u32[]{:S(2)}, u32[]{:S(2)}) async-start(f32[1,1024,256]{2,0,1:T(1,128)} %copy.12), calls=%async_computation | async-start | bytes 2097152 | tf_op jit(solution)/shard_map/all_to_all | solution.py:52
  425.1 184.0 %copy-start.3 = (f32[16,64,256]{2,1,0:T(8,128)}, f32[16,64,256]{2,1,0:T(8,128)S(1)}, u32[]{:S(2)}) copy-start(f32[16,64,256]{2,1,0:T(8,128)S(1)} %all_to_all.27) | copy-start | bytes 3145732
  425.1 27.5 %collective-permute-start = (f32[1,1024,256]{2,1,0:T(8,128)S(1)}, f32[1,1024,256]{2,1,0:T(8,128)S(1)}, u32[]{:S(2)}, u32[]{:S(2)}) collective-permute-start(f32[1,1024,256]{2,1,0:T(8,128)S(1)} %bitcast.112), channel_id=1, source_target_pairs={{0,1},{1,2},{2,3},{3,4},{4,5},{5,6},{6,7},{7,8},{8,9},{9,10},{10,1... | collective-permute-start | bytes 3145736 | tf_op jit(solution)/shard_map/ppermute | solution.py:77
  426.0 26.5 %collective-permute-start.1 = (f32[1,1024,256]{2,1,0:T(8,128)S(1)}, f32[1,1024,256]{2,1,0:T(8,128)S(1)}, u32[]{:S(2)}, u32[]{:S(2)}) collective-permute-start(f32[1,1024,256]{2,1,0:T(8,128)S(1)} %bitcast.113), channel_id=1, source_target_pairs={{0,15},{1,0},{2,1},{3,2},{4,3},{5,4},{6,5},{7,6},{8,7},{9,8},{10,9... | collective-permute-start | bytes 3145736 | tf_op jit(solution)/shard_map/ppermute | solution.py:82
  452.5 28.1 %collective-permute-start.2 = (f32[1,1024,256]{2,1,0:T(8,128)S(1)}, f32[1,1024,256]{2,1,0:T(8,128)S(1)}, u32[]{:S(2)}, u32[]{:S(2)}) collective-permute-start(f32[1,1024,256]{2,1,0:T(8,128)S(1)} %collective-permute-done), channel_id=1, source_target_pairs={{0,1},{1,2},{2,3},{3,4},{4,5},{5,6},{6,7},{7,8},{8,9},{9,10},{10,1... | collective-permute-start | bytes 3145736 | tf_op jit(solution)/shard_map/ppermute | solution.py:77
  452.6 28.1 %copy-start.4 = (f32[1,1024,256]{2,1,0:T(8,128)}, f32[1,1024,256]{2,1,0:T(8,128)S(1)}, u32[]{:S(2)}) copy-start(f32[1,1024,256]{2,1,0:T(8,128)S(1)} %collective-permute-done.1) | copy-start | bytes 3145732
  452.6 28.1 %collective-permute-start.3 = (f32[1,1024,256]{2,1,0:T(8,128)S(1)}, f32[1,1024,256]{2,1,0:T(8,128)S(1)}, u32[]{:S(2)}, u32[]{:S(2)}) collective-permute-start(f32[1,1024,256]{2,1,0:T(8,128)S(1)} %collective-permute-done.1), channel_id=1, source_target_pairs={{0,15},{1,0},{2,1},{3,2},{4,3},{5,4},{6,5},{7,6},{8,7},{9,8},{10,9... | collective-permute-start | bytes 3145736 | tf_op jit(solution)/shard_map/ppermute | solution.py:82
  480.7 79.9 %copy-start.8 = (f32[1,1024,256]{2,1,0:T(8,128)}, f32[1,1024,256]{2,1,0:T(8,128)S(1)}, u32[]{:S(2)}) copy-start(f32[1,1024,256]{2,1,0:T(8,128)S(1)} %collective-permute-done.2) | copy-start | bytes 3145732
  480.7 27.2 %collective-permute-start.4 = (f32[1,1024,256]{2,1,0:T(8,128)S(1)}, f32[1,1024,256]{2,1,0:T(8,128)S(1)}, u32[]{:S(2)}, u32[]{:S(2)}) collective-permute-start(f32[1,1024,256]{2,1,0:T(8,128)S(1)} %collective-permute-done.2), channel_id=1, source_target_pairs={{0,1},{1,2},{2,3},{3,4},{4,5},{5,6},{6,7},{7,8},{8,9},{9,10},{10,1... | collective-permute-start | bytes 3145736 | tf_op jit(solution)/shard_map/ppermute | solution.py:77
  480.7 27.2 %copy-start.14 = (f32[1,1024,256]{2,1,0:T(8,128)}, f32[1,1024,256]{2,1,0:T(8,128)S(1)}, u32[]{:S(2)}) copy-start(f32[1,1024,256]{2,1,0:T(8,128)S(1)} %collective-permute-done.3) | copy-start | bytes 3145732
  480.7 27.2 %collective-permute-start.5 = (f32[1,1024,256]{2,1,0:T(8,128)S(1)}, f32[1,1024,256]{2,1,0:T(8,128)S(1)}, u32[]{:S(2)}, u32[]{:S(2)}) collective-permute-start(f32[1,1024,256]{2,1,0:T(8,128)S(1)} %collective-permute-done.3), channel_id=1, source_target_pairs={{0,15},{1,0},{2,1},{3,2},{4,3},{5,4},{6,5},{7,6},{8,7},{9,8},{10,9... | collective-permute-start | bytes 3145736 | tf_op jit(solution)/shard_map/ppermute | solution.py:82
  507.9 4.9 copy-start.18
  507.9 26.3 %collective-permute-start.6 = (f32[1,1024,256]{2,1,0:T(8,128)S(1)}, f32[1,1024,256]{2,1,0:T(8,128)S(1)}, u32[]{:S(2)}, u32[]{:S(2)}) collective-permute-start(f32[1,1024,256]{2,1,0:T(8,128)S(1)} %collective-permute-done.4), channel_id=1, source_target_pairs={{0,1},{1,2},{2,3},{3,4},{4,5},{5,6},{6,7},{7,8},{8,9},{9,10},{10,1... | collective-permute-start | bytes 3145736 | tf_op jit(solution)/shard_map/ppermute | solution.py:77
  507.9 52.7 %copy-start.12 = (f32[1,1024,256]{2,1,0:T(8,128)}, f32[1,1024,256]{2,1,0:T(8,128)S(1)}, u32[]{:S(2)}) copy-start(f32[1,1024,256]{2,1,0:T(8,128)S(1)} %collective-permute-done.5) | copy-start | bytes 3145732
  507.9 27.3 %collective-permute-start.7 = (f32[1,1024,256]{2,1,0:T(8,128)S(1)}, f32[1,1024,256]{2,1,0:T(8,128)S(1)}, u32[]{:S(2)}, u32[]{:S(2)}) collective-permute-start(f32[1,1024,256]{2,1,0:T(8,128)S(1)} %collective-permute-done.5), channel_id=1, source_target_pairs={{0,15},{1,0},{2,1},{3,2},{4,3},{5,4},{6,5},{7,6},{8,7},{9,8},{10,9... | collective-permute-start | bytes 3145736 | tf_op jit(solution)/shard_map/ppermute | solution.py:82
  534.2 1.0 copy-start.6
  535.2 25.4 %collective-permute-start.8 = (f32[1,1024,256]{2,1,0:T(8,128)S(1)}, f32[1,1024,256]{2,1,0:T(8,128)S(1)}, u32[]{:S(2)}, u32[]{:S(2)}) collective-permute-start(f32[1,1024,256]{2,1,0:T(8,128)S(1)} %collective-permute-done.6), channel_id=1, source_target_pairs={{0,1},{1,2},{2,3},{3,4},{4,5},{5,6},{6,7},{7,8},{8,9},{9,10},{10,1... | collective-permute-start | bytes 3145736 | tf_op jit(solution)/shard_map/ppermute | solution.py:77
  535.2 25.4 %copy-start.10 = (f32[1,1024,256]{2,1,0:T(8,128)}, f32[1,1024,256]{2,1,0:T(8,128)S(1)}, u32[]{:S(2)}) copy-start(f32[1,1024,256]{2,1,0:T(8,128)S(1)} %collective-permute-done.7) | copy-start | bytes 3145732
  535.2 25.4 %collective-permute-start.9 = (f32[1,1024,256]{2,1,0:T(8,128)S(1)}, f32[1,1024,256]{2,1,0:T(8,128)}, u32[]{:S(2)}, u32[]{:S(2)}) collective-permute-start(f32[1,1024,256]{2,1,0:T(8,128)S(1)} %collective-permute-done.7), channel_id=1, source_target_pairs={{0,15},{1,0},{2,1},{3,2},{4,3},{5,4},{6,5},{7,6},{8,7},{9,8},{10,9... | collective-permute-start | bytes 3145736 | tf_op jit(solution)/shard_map/ppermute | solution.py:82
  560.6 4.9 copy-start.16
  560.6 24.6 %collective-permute-start.10 = (f32[1,1024,256]{2,1,0:T(8,128)S(1)}, f32[1,1024,256]{2,1,0:T(8,128)}, u32[]{:S(2)}, u32[]{:S(2)}) collective-permute-start(f32[1,1024,256]{2,1,0:T(8,128)S(1)} %collective-permute-done.8), channel_id=1, source_target_pairs={{0,1},{1,2},{2,3},{3,4},{4,5},{5,6},{6,7},{7,8},{8,9},{9,10},{10,1... | collective-permute-start | bytes 3145736 | tf_op jit(solution)/shard_map/ppermute | solution.py:77
  560.6 26.8 %collective-permute-start.11 = (f32[1,1024,256]{2,1,0:T(8,128)}, f32[1,1024,256]{2,1,0:T(8,128)}, u32[]{:S(2)}, u32[]{:S(2)}) collective-permute-start(f32[1,1024,256]{2,1,0:T(8,128)} %collective-permute-done.9), channel_id=1, source_target_pairs={{0,15},{1,0},{2,1},{3,2},{4,3},{5,4},{6,5},{7,6},{8,7},{9,8},{10,9... | collective-permute-start | bytes 3145736 | tf_op jit(solution)/shard_map/ppermute | solution.py:82
  585.2 23.9 %collective-permute-start.12 = (f32[1,1024,256]{2,1,0:T(8,128)}, f32[1,1024,256]{2,1,0:T(8,128)}, u32[]{:S(2)}, u32[]{:S(2)}) collective-permute-start(f32[1,1024,256]{2,1,0:T(8,128)} %collective-permute-done.10), channel_id=1, source_target_pairs={{0,1},{1,2},{2,3},{3,4},{4,5},{5,6},{6,7},{7,8},{8,9},{9,10},{10,1... | collective-permute-start | bytes 3145736 | tf_op jit(solution)/shard_map/ppermute | solution.py:77
  585.2 1.4 copy-start.5
  585.2 1.5 copy-start.9
  585.2 1.9 copy-start.15
  585.2 2.2 copy-start.19
  585.2 7.1 copy-start.13
  585.2 23.8 %copy-start.7 = (f32[1,1024,256]{2,1,0:T(8,128)S(1)}, f32[1,1024,256]{2,1,0:T(8,128)}, u32[]{:S(2)}) copy-start(f32[1,1024,256]{2,1,0:T(8,128)} %copy-done.6) | copy-start | bytes 3145732
  585.2 23.9 %copy-start.11 = (f32[1,1024,256]{2,1,0:T(8,128)S(1)}, f32[1,1024,256]{2,1,0:T(8,128)}, u32[]{:S(2)}) copy-start(f32[1,1024,256]{2,1,0:T(8,128)} %copy-done.10) | copy-start | bytes 3145732
  585.2 24.0 %copy-start.17 = (f32[1,1024,256]{2,1,0:T(8,128)S(1)}, f32[1,1024,256]{2,1,0:T(8,128)}, u32[]{:S(2)}) copy-start(f32[1,1024,256]{2,1,0:T(8,128)} %copy-done.16) | copy-start | bytes 3145732
  587.4 27.1 %collective-permute-start.13 = (f32[1,1024,256]{2,1,0:T(8,128)}, f32[1,1024,256]{2,1,0:T(8,128)S(1)}, u32[]{:S(2)}, u32[]{:S(2)}) collective-permute-start(f32[1,1024,256]{2,1,0:T(8,128)} %collective-permute-done.11), channel_id=1, source_target_pairs={{0,15},{1,0},{2,1},{3,2},{4,3},{5,4},{6,5},{7,6},{8,7},{9,8},{10,9... | collective-permute-start | bytes 3145736 | tf_op jit(solution)/shard_map/ppermute | solution.py:82
  609.0 22.8 %collective-permute-start.14 = (f32[1,1024,256]{2,1,0:T(8,128)}, f32[1,1024,256]{2,1,0:T(8,128)S(1)}, u32[]{:S(2)}, u32[]{:S(2)}) collective-permute-start(f32[1,1024,256]{2,1,0:T(8,128)} %collective-permute-done.12), channel_id=1, source_target_pairs={{0,1},{1,2},{2,3},{3,4},{4,5},{5,6},{6,7},{7,8},{8,9},{9,10},{10,1... | collective-permute-start | bytes 3145736 | tf_op jit(solution)/shard_map/ppermute | solution.py:77
  631.9 5.8 copy-start.1
  637.7 83.0 %copy-start.21 = (f32[256,256]{1,0:T(8,128)S(1)}, f32[256,256]{1,0:T(8,128)}, u32[]{:S(2)}) copy-start(f32[256,256]{1,0:T(8,128)} %param.21) | copy-start | bytes 786436
Sparse Core Ops, SparseCore 0:
  9.8 205.8 all-gather.1
